TPU v7x, 256 devices: a whole 4x4x8 slice. The times are simulated.
256 devices in a mesh: gx: 16 (over z, core), yz: 16 (over y, x).
Axes of the slice: x: 4, y: 4, z: 8, core: 2. Of those that a mesh axis runs over, the one named last changes fastest.
Arguments:
- loads: float32 [16, 294912], P(None, ('gx', 'yz')), may hold values from -30 to 30
- stiffness: bfloat16 [294912, 1152], P(('gx', 'yz')), may hold values from -1 to 16, as said below
- local_inverse: bfloat16 [294912, 1152], P(('gx', 'yz')), may hold values from -1 to 2, as said below
- coarse_basis: bfloat16 [24, 294912], P(None, ('gx', 'yz')), may hold values from -0.1875 to 0.1875
- coarse_inverse: bfloat16 [1024, 1024], replicated, may hold values from -1 to 2, as said below
- primal_index: int32 [256, 24], P(('gx', 'yz')), may hold values from 0 to 1023, as said below
- layer_counts: int32 [256, 2], P(('gx', 'yz')), may hold values from 0 to 144, as said below
- layer_index: int32 [256, 2, 144], P(('gx', 'yz')), may hold values from 0 to 1151, as said below
- across_counts: int32 [256, 16], P(('gx', 'yz')), may hold values from 0 to 48, as said below
- across_index: int32 [256, 16, 48], P(('gx', 'yz')), may hold values from 0 to 1151, as said below
Outputs:
- solution: float32 [16, 294912], P(None, ('gx', 'yz'))
- residual: float32 [16, 294912], P(None, ('gx', 'yz'))
- precond: float32 [16, 294912], P(None, ('gx', 'yz'))
Inputs may be any that keep to these rules, and one draw needn't show every extreme that they name: `stiffness`: each subdomain's block of 1152 rows is symmetric positive definite. `local_inverse`: each subdomain's block of 1152 rows is symmetric positive definite. `coarse_inverse`: symmetric positive definite. `primal_index`: the 24 entries of one subdomain are distinct. layer_counts[s, 1] equals layer_counts[s + 16, 0]; the lower count is 0 on the first layer and the upper count 0 on the last; for one position p across, drawn afresh, every two adjacent layers share exactly 144 dofs there. `layer_index`: entry j of subdomain s's upper list and entry j of subdomain s + 16's lower list name the same shared dof; entries past a count are 0; all list entries of one subdomain, layer and across lists together, are distinct. across_counts[g * 16 + p, q] equals across_counts[g * 16 + q, p]; it is 0 for q = p, exactly 48 for q = p + 1 and q = p - 1 (mod 16), and in each layer one subdomain shares exactly 48 with every other one. `across_index`: entry j of subdomain s's list toward t and entry j of t's list toward s name the same shared dof; entries past a count are 0.
All inputs are finite; a program needn't handle non-finite values.
Results may differ from a plain program's by a relative error of at most 0.025.
Values may be sent and summed in bfloat16 or wider, within the bound.
A program may use at most 64 MiB of HBM per device.

v0:
```python
import jax
import jax.numpy as jnp
from jax import lax
from jax.sharding import PartitionSpec as P

ITERS = 2


def extended(value, sides, width):
    for axis, dim in sides:
        count, length = (lax.axis_size(axis), value.shape[dim])
        up = [(i, (i + 1) % count) for i in range(count - 1)]
        down = [(j, i) for i, j in up]
        last = lax.slice_in_dim(value, length - width, length, axis=dim)
        initial = lax.slice_in_dim(value, 0, width, axis=dim)
        before = lax.ppermute(last, axis, up)
        after = lax.ppermute(initial, axis, down)
        value = jnp.concatenate([before, value, after], axis=dim)
    return value


def inner_product(left, right):
    return lax.dot_general(
        left,
        right,
        (((1,), (1,)), ((), ())),
        precision=lax.Precision.HIGHEST,
        preferred_element_type=jnp.float32,
    )


def spd_solve(matrix, right_side):
    lower = jnp.linalg.cholesky(matrix)
    middle = lax.linalg.triangular_solve(lower, right_side, left_side=True, lower=True)
    return lax.linalg.triangular_solve(lower, middle, left_side=True, lower=True, transpose_a=True)


def assemble(vector, lists):
    layer_list, layer_mask, across_list, across_mask = lists
    cases = vector.shape[0]
    outgoing = jnp.take(vector, layer_list, axis=1) * layer_mask[None]
    framed = extended(outgoing, (("gx", 1),), 1)
    sending = jnp.take(vector, across_list, axis=1) * across_mask[None]
    arrived = lax.all_to_all(
        sending.astype(jnp.bfloat16), "yz", split_axis=1, concat_axis=1, tiled=True
    ).astype(sending.dtype)
    summed = vector.at[:, across_list.reshape(-1)].add(arrived.reshape(cases, -1))
    summed = summed.at[:, layer_list[0]].add(framed[:, 0])
    return summed.at[:, layer_list[1]].add(framed[:, 3])


def dof_weight(length, lists):
    layer_list, layer_mask, across_list, across_mask = lists
    shared = jnp.zeros((length,), jnp.float32)
    shared = shared.at[layer_list.reshape(-1)].add(layer_mask.reshape(-1))
    shared = shared.at[across_list.reshape(-1)].add(across_mask.reshape(-1))
    return 1.0 / (1.0 + shared)


def precondition(residual, weight, local_inverse, coarse_basis, coarse_inverse, primal, lists):
    weighted = (weight[None] * residual).astype(jnp.bfloat16)
    local_part = jnp.dot(weighted, local_inverse, preferred_element_type=jnp.float32)
    coarse_terms = lax.dot_general(
        weighted, coarse_basis, (((1,), (1,)), ((), ())), preferred_element_type=jnp.float32
    )
    coarse_size = coarse_inverse.shape[0]
    selector = (primal[:, None] == jnp.arange(coarse_size)[None, :]).astype(jnp.float32)
    spread = jnp.dot(coarse_terms, selector, precision=lax.Precision.HIGHEST)
    coarse_total = lax.psum(spread, ("gx", "yz"))
    coarse_rhs = coarse_total.astype(jnp.bfloat16)
    row_count = coarse_size // lax.axis_size("gx")
    row_block = lax.dynamic_slice_in_dim(
        coarse_inverse, lax.axis_index("gx") * row_count, row_count, 0
    )
    own_rows = lax.dot_general(
        coarse_rhs, row_block, (((1,), (1,)), ((), ())), preferred_element_type=jnp.float32
    ).astype(jnp.bfloat16)
    coarse_solution = lax.all_gather(own_rows, "gx", axis=1, tiled=True)
    picked = jnp.take(coarse_solution, primal, axis=1)
    coarse_part = jnp.dot(picked, coarse_basis, preferred_element_type=jnp.float32)
    assembled = assemble(weight[None] * (local_part + coarse_part), lists)
    gram = lax.psum(inner_product(weight[None] * assembled, residual), ("gx", "yz"))
    return (assembled, gram)


def per_device(
    loads,
    stiffness,
    local_inverse,
    coarse_basis,
    coarse_inverse,
    primal_index,
    layer_counts,
    layer_index,
    across_counts,
    across_index,
):
    layer_list = layer_index[0]
    across_list = across_index[0]
    layer_mask = (jnp.arange(layer_list.shape[1])[None, :] < layer_counts[0][:, None]).astype(
        jnp.float32
    )
    across_mask = (jnp.arange(across_list.shape[1])[None, :] < across_counts[0][:, None]).astype(
        jnp.float32
    )
    lists = (layer_list, layer_mask, across_list, across_mask)
    weight = dof_weight(loads.shape[1], lists)
    primal = primal_index[0]

    def apply_preconditioner(current):
        return precondition(
            current, weight, local_inverse, coarse_basis, coarse_inverse, primal, lists
        )

    residual = assemble(loads, lists)
    solution = jnp.zeros_like(residual)
    precond, product = apply_preconditioner(residual)
    direction = precond
    for iteration in range(ITERS):
        stiff_image = jnp.dot(
            direction.astype(jnp.bfloat16), stiffness, preferred_element_type=jnp.float32
        )
        curvature = lax.psum(inner_product(direction, stiff_image), ("gx", "yz"))
        image = assemble(stiff_image, lists)
        alpha = spd_solve(curvature, product)
        solution = solution + jnp.dot(alpha.T, direction, precision=lax.Precision.HIGHEST)
        residual = residual - jnp.dot(alpha.T, image, precision=lax.Precision.HIGHEST)
        precond, product_next = apply_preconditioner(residual)
        if iteration + 1 < ITERS:
            beta = spd_solve(product, product_next)
            direction = precond + jnp.dot(beta.T, direction, precision=lax.Precision.HIGHEST)
        product = product_next
    return (solution, residual, precond)


def solution(mesh):
    in_specs = (
        P(None, ("gx", "yz")),
        P(("gx", "yz"), None),
        P(("gx", "yz"), None),
        P(None, ("gx", "yz")),
        P(),
        P(("gx", "yz"), None),
        P(("gx", "yz"), None),
        P(("gx", "yz"), None, None),
        P(("gx", "yz"), None),
        P(("gx", "yz"), None, None),
    )
    out_specs = (P(None, ("gx", "yz")), P(None, ("gx", "yz")), P(None, ("gx", "yz")))
    return jax.shard_map(
        per_device, mesh=mesh, in_specs=in_specs, out_specs=out_specs, check_vma=False
    )
```

profile of v0, /device:TPU:1, one launch (start us, length us, event | category | flops | bytes accessed | tf_op | source)
XLA Modules:
  0.0 816.1 jit_solution(10036473766111364378)
XLA Ops:
  5.4 5.1 collective-permute-start.1
  18.3 6.5 all-to-all-start
  25.8 3.6 scatter_custom_fusion
  29.4 5.6 scatter_fusion
  35.5 7.8 scatter_fusion.1
  43.3 3.5 scatter_custom_fusion.3
  46.8 3.6 scatter_custom_fusion.4
  52.1 79.4 %psum.49 = bf16[16,1024]{1,0:T(8,128)(2,1)S(1)} all-reduce(f32[16,1024]{1,0:T(8,128)S(1)} %fusion.19), channel_id=1, replica_groups=mesh['gx'=16,'yz'=16] {'gx','yz'}, use_global_device_ids=true, to_apply=%region_5.8 | all-reduce | flops 16384 | bytes 98304 | tf_op jit(solution)/shard_map/psum | solution.py:69
  132.5 16.6 %all-gather = bf16[16,64,16]{1,2,0:T(8,128)(2,1)S(1)} all-gather(bf16[1,64,16]{1,2,0:T(8,128)(2,1)S(1)} %fusion.3), channel_id=1, replica_groups=mesh['gx'=16,'yz'=16] {'gx'}, dimensions={0}, use_global_device_ids=true | all-gather | bytes 34816 | tf_op jit(solution)/shard_map/all_gather | solution.py:78
  160.1 3.5 all-to-all-start.1
  167.1 3.0 collective-permute-start.3
  172.8 7.4 scatter_fusion.2
  188.8 2.8 gather_fusion.6
  191.6 3.3 gather_fusion.5
  197.0 76.2 %all-reduce = (f32[16,16]{0,1:T(8,128)S(1)}, f32[16,16]{0,1:T(8,128)S(1)}) all-reduce(f32[16,16]{0,1:T(8,128)S(1)} %fusion.46, f32[16,16]{0,1:T(8,128)} %fusion.117), channel_id=1, replica_groups=mesh['gx'=16,'yz'=16] {'gx','yz'}, use_global_device_ids=true, to_apply=%region_12.17 | all-reduce | flops 512 | bytes 4096 | tf_op jit(solution)/shard_map/psum | solution.py:82
  283.7 3.0 collective-permute-start.4
  290.2 3.5 all-to-all-start.2
  294.3 5.8 all-to-all-done.2
  302.8 8.2 %scatter_fusion.3 = f32[16,1152]{0,1:T(8,128)} fusion(f32[16,1152]{0,1:T(8,128)} %copy.143, s32[768]{0:T(1024)S(1)} %fusion.94, f32[768,16]{1,0:T(8,128)} %copy.144), kind=kCustom, calls=%fused_computation.23 | custom fusion | flops 12288 | bytes 150528 | tf_op jit(solution)/shard_map/scatter-add | solution.py:47
  311.0 3.5 scatter_custom_fusion.9
  314.5 3.8 scatter_custom_fusion.10
  321.5 73.8 %psum.52 = bf16[16,1024]{1,0:T(8,128)(2,1)} all-reduce(f32[16,1024]{1,0:T(8,128)S(1)} %fusion.18), channel_id=1, replica_groups=mesh['gx'=16,'yz'=16] {'gx','yz'}, use_global_device_ids=true, to_apply=%region_16.0 | all-reduce | flops 16384 | bytes 98304 | tf_op jit(solution)/shard_map/psum | solution.py:69
  396.4 17.0 %all-gather.1 = bf16[16,64,16]{1,2,0:T(8,128)(2,1)S(1)} all-gather(bf16[1,64,16]{1,2,0:T(8,128)(2,1)S(1)} %fusion.4), channel_id=1, replica_groups=mesh['gx'=16,'yz'=16] {'gx'}, dimensions={0}, use_global_device_ids=true | all-gather | bytes 34816 | tf_op jit(solution)/shard_map/all_gather | solution.py:78
  421.3 3.3 gather_fusion.8
  428.4 3.5 collective-permute-start.6
  435.4 3.5 all-to-all-start.3
  441.4 4.1 all-to-all-done.3
  448.3 8.2 %scatter_fusion.4 = f32[16,1152]{0,1:T(8,128)} fusion(f32[16,1152]{0,1:T(8,128)} %copy.152, s32[768]{0:T(1024)S(1)} %fusion.94, f32[768,16]{1,0:T(8,128)} %copy.153), kind=kCustom, calls=%fused_computation.26 | custom fusion | flops 12288 | bytes 150528 | tf_op jit(solution)/shard_map/scatter-add | solution.py:47
  456.5 3.5 scatter_custom_fusion.12
  460.0 3.6 scatter_custom_fusion.13
  465.1 72.7 %psum.53 = f32[16,16]{1,0:T(8,128)S(1)} all-reduce(f32[16,16]{1,0:T(8,128)S(1)} %fusion.44), channel_id=1, replica_groups=mesh['gx'=16,'yz'=16] {'gx','yz'}, use_global_device_ids=true, to_apply=%region_20.27 | all-reduce | flops 256 | bytes 2048 | tf_op jit(solution)/shard_map/psum | solution.py:82
  546.1 3.3 gather_fusion.10
  549.4 73.5 %psum.54 = f32[16,16]{0,1:T(8,128)S(1)} all-reduce(f32[16,16]{0,1:T(8,128)} %fusion.118), channel_id=1, replica_groups=mesh['gx'=16,'yz'=16] {'gx','yz'}, use_global_device_ids=true, to_apply=%region_21.28 | all-reduce | flops 256 | bytes 2048 | tf_op jit(solution)/shard_map/psum | solution.py:123
  633.0 3.4 collective-permute-start.8
  639.8 4.4 all-to-all-start.4
  645.2 5.7 all-to-all-done.4
  654.3 8.2 %scatter_fusion.5 = f32[16,1152]{0,1:T(8,128)} fusion(f32[16,1152]{0,1:T(8,128)} %copy.163, s32[768]{0:T(1024)S(1)} %fusion.94, f32[768,16]{1,0:T(8,128)} %copy.164), kind=kCustom, calls=%fused_computation.29 | custom fusion | flops 12288 | bytes 150528 | tf_op jit(solution)/shard_map/scatter-add | solution.py:47
  662.5 3.5 scatter_custom_fusion.15
  666.0 3.6 scatter_custom_fusion.16
  673.5 73.6 %psum.55 = bf16[16,1024]{1,0:T(8,128)(2,1)} all-reduce(f32[16,1024]{1,0:T(8,128)} %fusion.17), channel_id=1, replica_groups=mesh['gx'=16,'yz'=16] {'gx','yz'}, use_global_device_ids=true, to_apply=%region_25.32 | all-reduce | flops 16384 | bytes 98304 | tf_op jit(solution)/shard_map/psum | solution.py:69
  748.2 17.6 %all-gather.2 = bf16[16,64,16]{1,2,0:T(8,128)(2,1)} all-gather(bf16[1,64,16]{1,2,0:T(8,128)(2,1)S(1)} %fusion.5), channel_id=1, replica_groups=mesh['gx'=16,'yz'=16] {'gx'}, dimensions={0}, use_global_device_ids=true | all-gather | bytes 34816 | tf_op jit(solution)/shard_map/all_gather | solution.py:78
  776.0 3.3 gather_fusion.13
  783.1 3.5 collective-permute-start.10
  788.6 3.7 all-to-all-start.5
  794.2 4.4 all-to-all-done.5
  799.1 7.8 scatter_fusion.6
  806.9 3.5 scatter_custom_fusion.18
  810.4 3.6 scatter_custom_fusion.19
  (205 shorter events, 139.0 us)
Async XLA Ops:
  0.6 148.5 %copy-start = (bf16[1152,1152]{1,0:T(8,128)(2,1)S(1)}, bf16[1152,1152]{1,0:T(8,128)(2,1)}, u32[]{:S(2)}) copy-start(bf16[1152,1152]{1,0:T(8,128)(2,1)} %param.23) | copy-start | bytes 7962628
  0.6 24.7 %copy-start.10 = (s32[1,2,144]{2,1,0:T(2,128)S(1)}, s32[1,2,144]{2,1,0:T(2,128)}, u32[]{:S(2)}) copy-start(s32[1,2,144]{2,1,0:T(2,128)} %param.28) | copy-start | bytes 3460
  0.7 24.8 %copy-start.6 = (s32[1,16,48]{2,1,0:T(8,128)S(1)}, s32[1,16,48]{2,1,0:T(8,128)}, u32[]{:S(2)}) copy-start(s32[1,16,48]{2,1,0:T(8,128)} %param.30) | copy-start | bytes 9220
  0.7 24.1 %copy-start.12 = (s32[1,24]{1,0:T(1,128)S(1)}, s32[1,24]{1,0:T(1,128)}, u32[]{:S(2)}) copy-start(s32[1,24]{1,0:T(1,128)} %param.26) | copy-start | bytes 292
  1.6 11.6 %copy-start.7 = (s32[1024]{0:T(1024)}, s32[1024]{0:T(1024)S(1)}, u32[]{:S(2)}) copy-start(s32[1024]{0:T(1024)S(1)} %pad_clamp_fusion.1) | copy-start | bytes 12292
  2.4 10.9 %copy-start.8 = (pred[2,144]{1,0:T(4,128)(4,1)}, pred[2,144]{1,0:T(4,128)(4,1)S(1)}, u32[]{:S(2)}) copy-start(pred[2,144]{1,0:T(4,128)(4,1)S(1)} %get-tuple-element.39) | copy-start | bytes 868
  3.5 22.2 %copy-start.1 = (f32[16,1152]{0,1:T(8,128)}, f32[16,1152]{0,1:T(8,128)S(1)}, u32[]{:S(2)}) copy-start(f32[16,1152]{0,1:T(8,128)S(1)} %copy.124) | copy-start | bytes 221188
  5.4 41.4 %collective-permute-start.1 = (f32[16,1,144]{0,2,1:T(8,128)}, f32[16,1,144]{0,2,1:T(8,128)}, u32[]{:S(2)}, u32[]{:S(2)}) collective-permute-start(f32[16,1,144]{0,2,1:T(8,128)} %get-tuple-element.33), channel_id=1, source_target_pairs={{16,0},{32,16},{48,32},{64,48},{80,64},{96,80},{112,96},{128,112},... | collective-permute-start | bytes 27656 | tf_op jit(solution)/shard_map/ppermute | solution.py:17
  10.5 32.8 %collective-permute-start = (f32[16,1,144]{0,2,1:T(8,128)}, f32[16,1,144]{0,2,1:T(8,128)}, u32[]{:S(2)}, u32[]{:S(2)}) collective-permute-start(f32[16,1,144]{0,2,1:T(8,128)} %get-tuple-element.34), channel_id=1, source_target_pairs={{0,16},{16,32},{32,48},{48,64},{64,80},{80,96},{96,112},{112,128},... | collective-permute-start | bytes 27656 | tf_op jit(solution)/shard_map/ppermute | solution.py:16
  18.3 16.8 %all-to-all-start = ((bf16[16,2,384]{2,1,0:T(2,128)(2,1)}), bf16[16,2,384]{2,1,0:T(2,128)(2,1)S(1)}, u32[]{:S(2)}, u32[]{:S(2)}) async-start(bf16[16,2,384]{2,1,0:T(2,128)(2,1)} %reshape.687), calls=%async_computation | async-start | bytes 49152 | tf_op jit(solution)/shard_map/all_to_all | solution.py:44
  25.5 17.8 %copy-start.16 = (s32[144,1]{0,1:T(1,128)}, s32[144,1]{0,1:T(1,128)S(1)}, u32[]{:S(2)}) copy-start(s32[144,1]{0,1:T(1,128)S(1)} %get-tuple-element.36) | copy-start | bytes 1732
  25.5 21.3 %copy-start.15 = (s32[144,1]{0,1:T(1,128)}, s32[144,1]{0,1:T(1,128)S(1)}, u32[]{:S(2)}) copy-start(s32[144,1]{0,1:T(1,128)S(1)} %get-tuple-element.35) | copy-start | bytes 1732
  35.0 16.7 %copy-start.2 = (bf16[24,1152]{1,0:T(8,128)(2,1)S(1)}, bf16[24,1152]{1,0:T(8,128)(2,1)}, u32[]{:S(2)}) copy-start(bf16[24,1152]{1,0:T(8,128)(2,1)} %param.24) | copy-start | bytes 165892
  35.0 16.8 %copy-start.13 = (s32[1,24]{1,0:T(1,128)S(1)}, s32[1,24]{1,0:T(1,128)}, u32[]{:S(2)}) copy-start(s32[1,24]{1,0:T(1,128)} %param.26) | copy-start | bytes 292
  35.0 114.7 %copy-start.11 = (s32[1024]{0:T(1024)}, s32[1024]{0:T(1024)S(1)}, u32[]{:S(2)}) copy-start(s32[1024]{0:T(1024)S(1)} %pad_clamp_fusion) | copy-start | bytes 12292
  46.8 103.6 %copy-start.14 = (pred[24]{0:T(512)(128)(4,1)S(1)}, pred[24]{0:T(512)(128)(4,1)}, u32[]{:S(2)}) copy-start(pred[24]{0:T(512)(128)(4,1)} %compare_and_fusion.2) | copy-start | bytes 76
  160.1 10.0 %all-to-all-start.1 = ((bf16[16,2,384]{2,1,0:T(2,128)(2,1)}), bf16[16,2,384]{2,1,0:T(2,128)(2,1)S(1)}, u32[]{:S(2)}, u32[]{:S(2)}) async-start(bf16[16,2,384]{2,1,0:T(2,128)(2,1)} %reshape.689), calls=%async_computation.1 | async-start | bytes 49152 | tf_op jit(solution)/shard_map/all_to_all | solution.py:44
  165.2 15.1 %collective-permute-start.2 = (f32[16,1,144]{0,2,1:T(8,128)}, f32[16,1,144]{0,2,1:T(8,128)}, u32[]{:S(2)}, u32[]{:S(2)}) collective-permute-start(f32[16,1,144]{0,2,1:T(8,128)} %get-tuple-element.32), channel_id=1, source_target_pairs={{0,16},{16,32},{32,48},{48,64},{64,80},{80,96},{96,112},{112,128},... | collective-permute-start | bytes 27656 | tf_op jit(solution)/shard_map/ppermute | solution.py:16
  167.1 15.1 %collective-permute-start.3 = (f32[16,1,144]{0,2,1:T(8,128)}, f32[16,1,144]{0,2,1:T(8,128)}, u32[]{:S(2)}, u32[]{:S(2)}) collective-permute-start(f32[16,1,144]{0,2,1:T(8,128)} %get-tuple-element.31), channel_id=1, source_target_pairs={{16,0},{32,16},{48,32},{64,48},{80,64},{96,80},{112,96},{128,112},... | collective-permute-start | bytes 27656 | tf_op jit(solution)/shard_map/ppermute | solution.py:17
  277.8 42.2 %copy-start.4 = (f32[16,16]{1,0:T(8,128)}, f32[16,16]{1,0:T(8,128)S(1)}, u32[]{:S(2)}) copy-start(f32[16,16]{1,0:T(8,128)S(1)} %fusion.79) | copy-start | bytes 3076
  279.2 11.0 %copy-start.9 = (f32[16,16]{1,0:T(8,128)}, f32[16,16]{1,0:T(8,128)S(1)}, u32[]{:S(2)}) copy-start(f32[16,16]{1,0:T(8,128)S(1)} %cholesky.70) | copy-start | bytes 3076
  281.0 33.5 %collective-permute-start.5 = (f32[16,1,144]{0,2,1:T(8,128)}, f32[16,1,144]{0,2,1:T(8,128)}, u32[]{:S(2)}, u32[]{:S(2)}) collective-permute-start(f32[16,1,144]{0,2,1:T(8,128)} %get-tuple-element.29), channel_id=1, source_target_pairs={{16,0},{32,16},{48,32},{64,48},{80,64},{96,80},{112,96},{128,112},... | collective-permute-start | bytes 27656 | tf_op jit(solution)/shard_map/ppermute | solution.py:17
  283.7 27.3 %collective-permute-start.4 = (f32[16,1,144]{0,2,1:T(8,128)}, f32[16,1,144]{0,2,1:T(8,128)}, u32[]{:S(2)}, u32[]{:S(2)}) collective-permute-start(f32[16,1,144]{0,2,1:T(8,128)} %get-tuple-element.30), channel_id=1, source_target_pairs={{0,16},{16,32},{32,48},{48,64},{64,80},{80,96},{96,112},{112,128},... | collective-permute-start | bytes 27656 | tf_op jit(solution)/shard_map/ppermute | solution.py:16
  290.2 9.9 %all-to-all-start.2 = ((bf16[16,2,384]{2,1,0:T(2,128)(2,1)}), bf16[16,2,384]{2,1,0:T(2,128)(2,1)S(1)}, u32[]{:S(2)}, u32[]{:S(2)}) async-start(bf16[16,2,384]{2,1,0:T(2,128)(2,1)} %reshape.691), calls=%async_computation.2 | async-start | bytes 49152 | tf_op jit(solution)/shard_map/all_to_all | solution.py:44
  426.4 33.6 %collective-permute-start.7 = (f32[16,1,144]{0,2,1:T(8,128)}, f32[16,1,144]{0,2,1:T(8,128)}, u32[]{:S(2)}, u32[]{:S(2)}) collective-permute-start(f32[16,1,144]{0,2,1:T(8,128)} %get-tuple-element.27), channel_id=1, source_target_pairs={{16,0},{32,16},{48,32},{64,48},{80,64},{96,80},{112,96},{128,112},... | collective-permute-start | bytes 27656 | tf_op jit(solution)/shard_map/ppermute | solution.py:17
  428.4 28.0 %collective-permute-start.6 = (f32[16,1,144]{0,2,1:T(8,128)}, f32[16,1,144]{0,2,1:T(8,128)}, u32[]{:S(2)}, u32[]{:S(2)}) collective-permute-start(f32[16,1,144]{0,2,1:T(8,128)} %get-tuple-element.28), channel_id=1, source_target_pairs={{0,16},{16,32},{32,48},{48,64},{64,80},{80,96},{96,112},{112,128},... | collective-permute-start | bytes 27656 | tf_op jit(solution)/shard_map/ppermute | solution.py:16
  435.4 10.1 %all-to-all-start.3 = ((bf16[16,2,384]{2,1,0:T(2,128)(2,1)}), bf16[16,2,384]{2,1,0:T(2,128)(2,1)S(1)}, u32[]{:S(2)}, u32[]{:S(2)}) async-start(bf16[16,2,384]{2,1,0:T(2,128)(2,1)} %reshape.693), calls=%async_computation.3 | async-start | bytes 49152 | tf_op jit(solution)/shard_map/all_to_all | solution.py:44
  537.8 0.6 copy-start.5
  630.4 35.6 %collective-permute-start.9 = (f32[16,1,144]{0,2,1:T(8,128)}, f32[16,1,144]{0,2,1:T(8,128)}, u32[]{:S(2)}, u32[]{:S(2)}) collective-permute-start(f32[16,1,144]{0,2,1:T(8,128)} %get-tuple-element.25), channel_id=1, source_target_pairs={{16,0},{32,16},{48,32},{64,48},{80,64},{96,80},{112,96},{128,112},... | collective-permute-start | bytes 27656 | tf_op jit(solution)/shard_map/ppermute | solution.py:17
  633.0 29.5 %collective-permute-start.8 = (f32[16,1,144]{0,2,1:T(8,128)}, f32[16,1,144]{0,2,1:T(8,128)}, u32[]{:S(2)}, u32[]{:S(2)}) collective-permute-start(f32[16,1,144]{0,2,1:T(8,128)} %get-tuple-element.26), channel_id=1, source_target_pairs={{0,16},{16,32},{32,48},{48,64},{64,80},{80,96},{96,112},{112,128},... | collective-permute-start | bytes 27656 | tf_op jit(solution)/shard_map/ppermute | solution.py:16
  639.8 11.0 %all-to-all-start.4 = ((bf16[16,2,384]{2,1,0:T(2,128)(2,1)}), bf16[16,2,384]{2,1,0:T(2,128)(2,1)}, u32[]{:S(2)}, u32[]{:S(2)}) async-start(bf16[16,2,384]{2,1,0:T(2,128)(2,1)} %reshape.695), calls=%async_computation.4 | async-start | bytes 49152 | tf_op jit(solution)/shard_map/all_to_all | solution.py:44
  671.3 108.0 %copy-start.3 = (f32[16,1152]{1,0:T(8,128)}, f32[16,1152]{1,0:T(8,128)S(1)}, u32[]{:S(2)}) copy-start(f32[16,1152]{1,0:T(8,128)S(1)} %convolution_subtract_fusion) | copy-start | bytes 221188
  781.1 29.3 %collective-permute-start.11 = (f32[16,1,144]{0,2,1:T(8,128)}, f32[16,1,144]{0,2,1:T(8,128)}, u32[]{:S(2)}, u32[]{:S(2)}) collective-permute-start(f32[16,1,144]{0,2,1:T(8,128)} %get-tuple-element.23), channel_id=1, source_target_pairs={{16,0},{32,16},{48,32},{64,48},{80,64},{96,80},{112,96},{128,112},... | collective-permute-start | bytes 27656 | tf_op jit(solution)/shard_map/ppermute | solution.py:17
  783.1 23.8 %collective-permute-start.10 = (f32[16,1,144]{0,2,1:T(8,128)}, f32[16,1,144]{0,2,1:T(8,128)}, u32[]{:S(2)}, u32[]{:S(2)}) collective-permute-start(f32[16,1,144]{0,2,1:T(8,128)} %get-tuple-element.24), channel_id=1, source_target_pairs={{0,16},{16,32},{32,48},{48,64},{64,80},{80,96},{96,112},{112,128},... | collective-permute-start | bytes 27656 | tf_op jit(solution)/shard_map/ppermute | solution.py:16
  788.6 10.1 %all-to-all-start.5 = ((bf16[16,2,384]{2,1,0:T(2,128)(2,1)}), bf16[16,2,384]{2,1,0:T(2,128)(2,1)S(1)}, u32[]{:S(2)}, u32[]{:S(2)}) async-start(bf16[16,2,384]{2,1,0:T(2,128)(2,1)} %reshape.697), calls=%async_computation.5 | async-start | bytes 49152 | tf_op jit(solution)/shard_map/all_to_all | solution.py:44
where the time goes:
time: 829 us; the launch traced here: 816 us
  blocking collectives  500 us (60%)
  other arithmetic  123 us (15%)
  local copies, waits for them, and re-layouts  83 us (10%)
  starting transfers between devices  59.8 us (7%)
  matrix products  28.6 us (3%)
  waiting for transfers between devices  20.1 us (2%)
    psum x3, blocking collectives, precondition(): coarse_total = lax.psum(spread, ('gx', 'yz'))  227 us
    psum x2, blocking collectives, precondition(): lax.psum(inner_product(weight[None] * assembled, residual), ('gx', 'yz'))  149 us
    psum x1, blocking collectives, per_device(): curvature = lax.psum(inner_product(direction, stiff_image), ('gx', 'yz'))  73.5 us
    all_gather x3, blocking collectives, precondition(): coarse_solution = lax.all_gather(own_rows, 'gx', axis=1, tiled=True)  51.2 us
    scatter-add x6, other arithmetic, assemble(): vector.at[:, across_list.reshape(-1)].add(arrived.reshape(cases, -1))  47.6 us
    gather x12, local copies, waits for them, and re-layouts, assemble(): sending = jnp.take(vector, across_list, axis=1) * across_mask[None]  27.3 us
    all_to_all x6, starting transfers between devices, assemble(): lax.all_to_all(sending.astype(jnp.bfloat16), 'yz', split_axis=1, concat_a...  25.1 us
    scatter-add x6, other arithmetic, assemble(): return summed.at[:, layer_list[1]].add(framed[:, 3])  20.3 us
  transfers between devices with their start and end apart: 18, of which 4 were waited for; matrix products, arithmetic and copies ran while one was open for 14% of the time, Pallas kernels for 0%

commit v1 on v0

--- a/solution.py
+++ b/solution.py
@@ -79,7 +79,9 @@
     picked = jnp.take(coarse_solution, primal, axis=1)
     coarse_part = jnp.dot(picked, coarse_basis, preferred_element_type=jnp.float32)
     assembled = assemble(weight[None] * (local_part + coarse_part), lists)
-    gram = lax.psum(inner_product(weight[None] * assembled, residual), ("gx", "yz"))
+    gram = jnp.sum(
+        lax.all_gather(inner_product(weight[None] * assembled, residual), ("gx", "yz")), axis=0
+    )
     return (assembled, gram)
 
 

time: 829 us -> 999 us (1.21)
  blocking collectives: 500 us -> 693 us
  waiting for transfers between devices: 20.1 us -> 0.05 us
    all_gather x0 -> x2, blocking collectives: none -> 254 us  [precondition(): lax.all_gather(inner_product(weight[None] * assembled, residual), ('gx',...]
    psum x2 -> x0, blocking collectives: 149 us -> none  [precondition(): lax.psum(inner_product(weight[None] * assembled, residual), ('gx', 'yz'))]
    psum x1 -> x2, blocking collectives: 73.5 us -> 161 us  [per_device(): curvature = lax.psum(inner_product(direction, stiff_image), ('gx', 'yz'))]
    all_to_all x6, waiting for transfers between devices: 20 us -> 0.02 us  [assemble(): lax.all_to_all(sending.astype(jnp.bfloat16), 'yz', split_axis=1, concat_a...]
  transfers between devices with their start and end apart: 18 -> 18, of which waited for: 4 -> 0; matrix products, arithmetic and copies ran while one was open for 14% -> 12% of each run, Pallas kernels for 0% -> 0%
where the time goes in v1:
time: 999 us; the launch traced here: 986 us
  blocking collectives  693 us (69%)
  other arithmetic  125 us (13%)
  local copies, waits for them, and re-layouts  82.5 us (8%)
  starting transfers between devices  57.9 us (6%)
  matrix products  26.6 us (3%)
    all_gather x2, blocking collectives, precondition(): lax.all_gather(inner_product(weight[None] * assembled, residual), ('gx',...  254 us
    psum x3, blocking collectives, precondition(): coarse_total = lax.psum(spread, ('gx', 'yz'))  226 us
    psum x2, blocking collectives, per_device(): curvature = lax.psum(inner_product(direction, stiff_image), ('gx', 'yz'))  161 us
    all_gather x3, blocking collectives, precondition(): coarse_solution = lax.all_gather(own_rows, 'gx', axis=1, tiled=True)  51.6 us
    scatter-add x6, other arithmetic, assemble(): vector.at[:, across_list.reshape(-1)].add(arrived.reshape(cases, -1))  47.2 us
    gather x12, local copies, waits for them, and re-layouts, assemble(): sending = jnp.take(vector, across_list, axis=1) * across_mask[None]  27.3 us
    all_to_all x6, starting transfers between devices, assemble(): lax.all_to_all(sending.astype(jnp.bfloat16), 'yz', split_axis=1, concat_a...  26 us
    scatter-add x6, other arithmetic, assemble(): return summed.at[:, layer_list[1]].add(framed[:, 3])  20.1 us
  transfers between devices with their start and end apart: 18, of which 0 were waited for; matrix products, arithmetic and copies ran while one was open for 12% of the time, Pallas kernels for 0%

profile of v1, /device:TPU:1, one launch (start us, length us, event | category | flops | bytes accessed | tf_op | source)
XLA Modules:
  0.0 986.0 jit_solution(12008260489394033336)
XLA Ops:
  7.7 7.6 all-to-all-start
  17.4 4.4 collective-permute-start
  24.7 3.6 scatter_custom_fusion
  28.3 5.6 scatter_fusion
  34.4 7.8 scatter_fusion.1
  42.2 3.5 scatter_custom_fusion.3
  45.7 3.6 scatter_custom_fusion.4
  50.9 80.0 %psum.35 = bf16[16,1024]{1,0:T(8,128)(2,1)S(1)} all-reduce(f32[16,1024]{1,0:T(8,128)S(1)} %fusion.19), channel_id=1, replica_groups=mesh['gx'=16,'yz'=16] {'gx','yz'}, use_global_device_ids=true, to_apply=%region_5.8 | all-reduce | flops 16384 | bytes 98304 | tf_op jit(solution)/shard_map/psum | solution.py:69
  132.0 15.9 %all-gather.2 = bf16[16,64,16]{1,2,0:T(8,128)(2,1)S(1)} all-gather(bf16[1,64,16]{1,2,0:T(8,128)(2,1)S(1)} %fusion.3), channel_id=1, replica_groups=mesh['gx'=16,'yz'=16] {'gx'}, dimensions={0}, use_global_device_ids=true | all-gather | bytes 34816 | tf_op jit(solution)/shard_map/all_gather | solution.py:78
  157.1 3.5 all-to-all-start.1
  162.3 2.6 collective-permute-start.2
  169.9 7.1 scatter_fusion.2
  184.6 3.3 gather_fusion.5
  187.9 2.8 gather_fusion.6
  193.3 127.2 %all-gather = f32[4096,16]{1,0:T(8,128)} all-gather(f32[16,16]{1,0:T(8,128)S(1)} %fusion.46), channel_id=2, replica_groups=mesh['gx'=16,'yz'=16] {'gx','yz'}, dimensions={0}, use_global_device_ids=true | all-gather | bytes 263168 | tf_op jit(solution)/shard_map/all_gather | solution.py:83
  327.3 3.8 all-to-all-start.2
  334.8 3.7 collective-permute-start.5
  338.4 80.4 %psum.36 = f32[16,16]{0,1:T(8,128)S(1)} all-reduce(f32[16,16]{0,1:T(8,128)S(1)} %copy-done.11), channel_id=1, replica_groups=mesh['gx'=16,'yz'=16] {'gx','yz'}, use_global_device_ids=true, to_apply=%region_9.13 | all-reduce | flops 256 | bytes 2048 | tf_op jit(solution)/shard_map/psum | solution.py:125
  426.8 8.2 scatter_fusion.3
  435.0 3.5 scatter_custom_fusion.9
  438.5 3.6 scatter_custom_fusion.10
  445.3 73.2 %psum.37 = bf16[16,1024]{1,0:T(8,128)(2,1)} all-reduce(f32[16,1024]{1,0:T(8,128)S(1)} %fusion.18), channel_id=1, replica_groups=mesh['gx'=16,'yz'=16] {'gx','yz'}, use_global_device_ids=true, to_apply=%region_16.0 | all-reduce | flops 16384 | bytes 98304 | tf_op jit(solution)/shard_map/psum | solution.py:69
  519.6 17.0 %all-gather.3 = bf16[16,64,16]{1,2,0:T(8,128)(2,1)S(1)} all-gather(bf16[1,64,16]{1,2,0:T(8,128)(2,1)S(1)} %fusion.4), channel_id=1, replica_groups=mesh['gx'=16,'yz'=16] {'gx'}, dimensions={0}, use_global_device_ids=true | all-gather | bytes 34816 | tf_op jit(solution)/shard_map/all_gather | solution.py:78
  541.7 3.3 gather_fusion.8
  545.1 2.8 gather_fusion.9
  551.3 3.5 all-to-all-start.3
  556.6 2.8 collective-permute-start.6
  566.8 8.2 scatter_fusion.4
  575.0 3.9 scatter_custom_fusion.12
  578.9 3.6 scatter_custom_fusion.13
  584.0 127.3 %all-gather.1 = f32[4096,16]{1,0:T(8,128)} all-gather(f32[16,16]{1,0:T(8,128)S(1)} %fusion.44), channel_id=3, replica_groups=mesh['gx'=16,'yz'=16] {'gx','yz'}, dimensions={0}, use_global_device_ids=true | all-gather | bytes 263168 | tf_op jit(solution)/shard_map/all_gather | solution.py:83
  717.8 3.3 gather_fusion.10
  721.1 2.8 gather_fusion.11
  728.2 4.1 all-to-all-start.4
  736.0 3.3 collective-permute-start.9
  739.3 80.2 %psum.38 = f32[16,16]{0,1:T(8,128)S(1)} all-reduce(f32[16,16]{0,1:T(8,128)} %fusion.118), channel_id=1, replica_groups=mesh['gx'=16,'yz'=16] {'gx','yz'}, use_global_device_ids=true, to_apply=%region_21.28 | all-reduce | flops 256 | bytes 2048 | tf_op jit(solution)/shard_map/psum | solution.py:125
  829.0 8.2 scatter_fusion.5
  837.2 3.5 scatter_custom_fusion.15
  840.7 3.6 scatter_custom_fusion.16
  848.1 73.1 %psum.39 = bf16[16,1024]{1,0:T(8,128)(2,1)} all-reduce(f32[16,1024]{1,0:T(8,128)} %fusion.17), channel_id=1, replica_groups=mesh['gx'=16,'yz'=16] {'gx','yz'}, use_global_device_ids=true, to_apply=%region_25.32 | all-reduce | flops 16384 | bytes 98304 | tf_op jit(solution)/shard_map/psum | solution.py:69
  922.3 18.7 %all-gather.4 = bf16[16,64,16]{1,2,0:T(8,128)(2,1)} all-gather(bf16[1,64,16]{1,2,0:T(8,128)(2,1)S(1)} %fusion.5), channel_id=1, replica_groups=mesh['gx'=16,'yz'=16] {'gx'}, dimensions={0}, use_global_device_ids=true | all-gather | bytes 34816 | tf_op jit(solution)/shard_map/all_gather | solution.py:78
  948.4 3.3 gather_fusion.13
  951.8 2.8 gather_fusion.14
  956.5 3.5 all-to-all-start.5
  961.7 2.8 collective-permute-start.10
  969.0 7.8 scatter_fusion.6
  976.8 3.5 scatter_custom_fusion.18
  980.3 3.6 scatter_custom_fusion.19
  (216 shorter events, 129.3 us)
Async XLA Ops:
  0.6 147.4 %copy-start = (bf16[1152,1152]{1,0:T(8,128)(2,1)S(1)}, bf16[1152,1152]{1,0:T(8,128)(2,1)}, u32[]{:S(2)}) copy-start(bf16[1152,1152]{1,0:T(8,128)(2,1)} %param.23) | copy-start | bytes 7962628
  0.6 23.1 %copy-start.7 = (s32[1,16,48]{2,1,0:T(8,128)S(1)}, s32[1,16,48]{2,1,0:T(8,128)}, u32[]{:S(2)}) copy-start(s32[1,16,48]{2,1,0:T(8,128)} %param.30) | copy-start | bytes 9220
  0.7 14.7 %copy-start.13 = (s32[1,2,144]{2,1,0:T(2,128)S(1)}, s32[1,2,144]{2,1,0:T(2,128)}, u32[]{:S(2)}) copy-start(s32[1,2,144]{2,1,0:T(2,128)} %param.28) | copy-start | bytes 3460
  0.7 15.8 %copy-start.20 = (s32[1,2]{1,0:T(1,128)S(1)}, s32[1,2]{1,0:T(1,128)}, u32[]{:S(2)}) copy-start(s32[1,2]{1,0:T(1,128)} %param.27) | copy-start | bytes 28
  0.7 23.4 %copy-start.15 = (s32[1,24]{1,0:T(1,128)S(1)}, s32[1,24]{1,0:T(1,128)}, u32[]{:S(2)}) copy-start(s32[1,24]{1,0:T(1,128)} %param.26) | copy-start | bytes 292
  2.8 21.9 %copy-start.1 = (f32[16,1152]{0,1:T(8,128)}, f32[16,1152]{0,1:T(8,128)S(1)}, u32[]{:S(2)}) copy-start(f32[16,1152]{0,1:T(8,128)S(1)} %copy.121) | copy-start | bytes 221188
  7.7 26.2 %all-to-all-start = ((bf16[16,2,384]{2,1,0:T(2,128)(2,1)}), bf16[16,2,384]{2,1,0:T(2,128)(2,1)S(1)}, u32[]{:S(2)}, u32[]{:S(2)}) async-start(bf16[16,2,384]{2,1,0:T(2,128)(2,1)} %reshape.689), calls=%async_computation | async-start | bytes 49152 | tf_op jit(solution)/shard_map/all_to_all | solution.py:44
  15.4 8.7 copy-start.8
  16.6 17.3 %copy-start.9 = (pred[2,144]{1,0:T(4,128)(4,1)}, pred[2,144]{1,0:T(4,128)(4,1)S(1)}, u32[]{:S(2)}) copy-start(pred[2,144]{1,0:T(4,128)(4,1)S(1)} %get-tuple-element.37) | copy-start | bytes 868
  17.4 24.8 %collective-permute-start = (f32[16,1,144]{0,2,1:T(8,128)}, f32[16,1,144]{0,2,1:T(8,128)}, u32[]{:S(2)}, u32[]{:S(2)}) collective-permute-start(f32[16,1,144]{0,2,1:T(8,128)} %get-tuple-element.32), channel_id=1, source_target_pairs={{0,16},{16,32},{32,48},{48,64},{64,80},{80,96},{96,112},{112,128},... | collective-permute-start | bytes 27656 | tf_op jit(solution)/shard_map/ppermute | solution.py:16
  21.8 23.9 %collective-permute-start.1 = (f32[16,1,144]{0,2,1:T(8,128)}, f32[16,1,144]{0,2,1:T(8,128)}, u32[]{:S(2)}, u32[]{:S(2)}) collective-permute-start(f32[16,1,144]{0,2,1:T(8,128)} %get-tuple-element.31), channel_id=1, source_target_pairs={{16,0},{32,16},{48,32},{64,48},{80,64},{96,80},{112,96},{128,112},... | collective-permute-start | bytes 27656 | tf_op jit(solution)/shard_map/ppermute | solution.py:17
  23.8 18.4 %copy-start.19 = (s32[144,1]{0,1:T(1,128)}, s32[144,1]{0,1:T(1,128)S(1)}, u32[]{:S(2)}) copy-start(s32[144,1]{0,1:T(1,128)S(1)} %get-tuple-element.34) | copy-start | bytes 1732
  23.8 21.8 %copy-start.18 = (s32[144,1]{0,1:T(1,128)}, s32[144,1]{0,1:T(1,128)S(1)}, u32[]{:S(2)}) copy-start(s32[144,1]{0,1:T(1,128)S(1)} %get-tuple-element.33) | copy-start | bytes 1732
  33.9 16.6 %copy-start.2 = (bf16[24,1152]{1,0:T(8,128)(2,1)S(1)}, bf16[24,1152]{1,0:T(8,128)(2,1)}, u32[]{:S(2)}) copy-start(bf16[24,1152]{1,0:T(8,128)(2,1)} %param.24) | copy-start | bytes 165892
  33.9 16.8 %copy-start.16 = (s32[1,24]{1,0:T(1,128)S(1)}, s32[1,24]{1,0:T(1,128)}, u32[]{:S(2)}) copy-start(s32[1,24]{1,0:T(1,128)} %param.26) | copy-start | bytes 292
  34.0 114.5 %copy-start.14 = (s32[1024]{0:T(1024)}, s32[1024]{0:T(1024)S(1)}, u32[]{:S(2)}) copy-start(s32[1024]{0:T(1024)S(1)} %pad_clamp_fusion) | copy-start | bytes 12292
  45.7 103.4 %copy-start.17 = (pred[24]{0:T(512)(128)(4,1)S(1)}, pred[24]{0:T(512)(128)(4,1)}, u32[]{:S(2)}) copy-start(pred[24]{0:T(512)(128)(4,1)} %compare_and_fusion.2) | copy-start | bytes 76
  157.1 10.2 %all-to-all-start.1 = ((bf16[16,2,384]{2,1,0:T(2,128)(2,1)}), bf16[16,2,384]{2,1,0:T(2,128)(2,1)S(1)}, u32[]{:S(2)}, u32[]{:S(2)}) async-start(bf16[16,2,384]{2,1,0:T(2,128)(2,1)} %reshape.691), calls=%async_computation.1 | async-start | bytes 49152 | tf_op jit(solution)/shard_map/all_to_all | solution.py:44
  162.3 14.8 %collective-permute-start.2 = (f32[16,1,144]{0,2,1:T(8,128)}, f32[16,1,144]{0,2,1:T(8,128)}, u32[]{:S(2)}, u32[]{:S(2)}) collective-permute-start(f32[16,1,144]{0,2,1:T(8,128)} %get-tuple-element.30), channel_id=1, source_target_pairs={{0,16},{16,32},{32,48},{48,64},{64,80},{80,96},{96,112},{112,128},... | collective-permute-start | bytes 27656 | tf_op jit(solution)/shard_map/ppermute | solution.py:16
  164.9 14.1 %collective-permute-start.3 = (f32[16,1,144]{0,2,1:T(8,128)}, f32[16,1,144]{0,2,1:T(8,128)}, u32[]{:S(2)}, u32[]{:S(2)}) collective-permute-start(f32[16,1,144]{0,2,1:T(8,128)} %get-tuple-element.29), channel_id=1, source_target_pairs={{16,0},{32,16},{48,32},{64,48},{80,64},{96,80},{112,96},{128,112},... | collective-permute-start | bytes 27656 | tf_op jit(solution)/shard_map/ppermute | solution.py:17
  193.2 137.9 %copy-start.10 = (pred[2,144]{1,0:T(4,128)(4,1)S(1)}, pred[2,144]{1,0:T(4,128)(4,1)}, u32[]{:S(2)}) copy-start(pred[2,144]{1,0:T(4,128)(4,1)} %copy-done.9) | copy-start | bytes 868
  193.2 145.2 %copy-start.11 = (f32[16,16]{0,1:T(8,128)S(1)}, f32[16,16]{0,1:T(8,128)}, u32[]{:S(2)}) copy-start(f32[16,16]{0,1:T(8,128)} %fusion.117) | copy-start | bytes 3076
  323.8 3.5 copy-start.12
  327.3 96.8 %all-to-all-start.2 = ((bf16[16,2,384]{2,1,0:T(2,128)(2,1)}), bf16[16,2,384]{2,1,0:T(2,128)(2,1)S(1)}, u32[]{:S(2)}, u32[]{:S(2)}) async-start(bf16[16,2,384]{2,1,0:T(2,128)(2,1)} %reshape.693), calls=%async_computation.2 | async-start | bytes 49152 | tf_op jit(solution)/shard_map/all_to_all | solution.py:44
  332.8 102.1 %collective-permute-start.4 = (f32[16,1,144]{0,2,1:T(8,128)}, f32[16,1,144]{0,2,1:T(8,128)}, u32[]{:S(2)}, u32[]{:S(2)}) collective-permute-start(f32[16,1,144]{0,2,1:T(8,128)} %get-tuple-element.28), channel_id=1, source_target_pairs={{0,16},{16,32},{32,48},{48,64},{64,80},{80,96},{96,112},{112,128},... | collective-permute-start | bytes 27656 | tf_op jit(solution)/shard_map/ppermute | solution.py:16
  334.8 103.7 %collective-permute-start.5 = (f32[16,1,144]{0,2,1:T(8,128)}, f32[16,1,144]{0,2,1:T(8,128)}, u32[]{:S(2)}, u32[]{:S(2)}) collective-permute-start(f32[16,1,144]{0,2,1:T(8,128)} %get-tuple-element.27), channel_id=1, source_target_pairs={{16,0},{32,16},{48,32},{64,48},{80,64},{96,80},{112,96},{128,112},... | collective-permute-start | bytes 27656 | tf_op jit(solution)/shard_map/ppermute | solution.py:17
  423.4 20.6 %copy-start.4 = (f32[16,16]{1,0:T(8,128)}, f32[16,16]{1,0:T(8,128)S(1)}, u32[]{:S(2)}) copy-start(f32[16,16]{1,0:T(8,128)S(1)} %fusion.79) | copy-start | bytes 3076
  551.3 12.8 %all-to-all-start.3 = ((bf16[16,2,384]{2,1,0:T(2,128)(2,1)}), bf16[16,2,384]{2,1,0:T(2,128)(2,1)S(1)}, u32[]{:S(2)}, u32[]{:S(2)}) async-start(bf16[16,2,384]{2,1,0:T(2,128)(2,1)} %reshape.695), calls=%async_computation.3 | async-start | bytes 49152 | tf_op jit(solution)/shard_map/all_to_all | solution.py:44
  556.6 18.5 %collective-permute-start.6 = (f32[16,1,144]{0,2,1:T(8,128)}, f32[16,1,144]{0,2,1:T(8,128)}, u32[]{:S(2)}, u32[]{:S(2)}) collective-permute-start(f32[16,1,144]{0,2,1:T(8,128)} %get-tuple-element.26), channel_id=1, source_target_pairs={{0,16},{16,32},{32,48},{48,64},{64,80},{80,96},{96,112},{112,128},... | collective-permute-start | bytes 27656 | tf_op jit(solution)/shard_map/ppermute | solution.py:16
  559.3 19.6 %collective-permute-start.7 = (f32[16,1,144]{0,2,1:T(8,128)}, f32[16,1,144]{0,2,1:T(8,128)}, u32[]{:S(2)}, u32[]{:S(2)}) collective-permute-start(f32[16,1,144]{0,2,1:T(8,128)} %get-tuple-element.25), channel_id=1, source_target_pairs={{16,0},{32,16},{48,32},{64,48},{80,64},{96,80},{112,96},{128,112},... | collective-permute-start | bytes 27656 | tf_op jit(solution)/shard_map/ppermute | solution.py:17
  713.1 0.6 copy-start.5
  728.2 97.4 %all-to-all-start.4 = ((bf16[16,2,384]{2,1,0:T(2,128)(2,1)}), bf16[16,2,384]{2,1,0:T(2,128)(2,1)}, u32[]{:S(2)}, u32[]{:S(2)}) async-start(bf16[16,2,384]{2,1,0:T(2,128)(2,1)} %reshape.697), calls=%async_computation.4 | async-start | bytes 49152 | tf_op jit(solution)/shard_map/all_to_all | solution.py:44
  734.1 103.1 %collective-permute-start.8 = (f32[16,1,144]{0,2,1:T(8,128)}, f32[16,1,144]{0,2,1:T(8,128)}, u32[]{:S(2)}, u32[]{:S(2)}) collective-permute-start(f32[16,1,144]{0,2,1:T(8,128)} %get-tuple-element.24), channel_id=1, source_target_pairs={{0,16},{16,32},{32,48},{48,64},{64,80},{80,96},{96,112},{112,128},... | collective-permute-start | bytes 27656 | tf_op jit(solution)/shard_map/ppermute | solution.py:16
  736.0 104.7 %collective-permute-start.9 = (f32[16,1,144]{0,2,1:T(8,128)}, f32[16,1,144]{0,2,1:T(8,128)}, u32[]{:S(2)}, u32[]{:S(2)}) collective-permute-start(f32[16,1,144]{0,2,1:T(8,128)} %get-tuple-element.23), channel_id=1, source_target_pairs={{16,0},{32,16},{48,32},{64,48},{80,64},{96,80},{112,96},{128,112},... | collective-permute-start | bytes 27656 | tf_op jit(solution)/shard_map/ppermute | solution.py:17
  824.7 0.6 copy-start.6
  846.0 105.8 %copy-start.3 = (f32[16,1152]{1,0:T(8,128)}, f32[16,1152]{1,0:T(8,128)S(1)}, u32[]{:S(2)}) copy-start(f32[16,1152]{1,0:T(8,128)S(1)} %convolution_subtract_fusion) | copy-start | bytes 221188
  956.5 12.1 %all-to-all-start.5 = ((bf16[16,2,384]{2,1,0:T(2,128)(2,1)}), bf16[16,2,384]{2,1,0:T(2,128)(2,1)S(1)}, u32[]{:S(2)}, u32[]{:S(2)}) async-start(bf16[16,2,384]{2,1,0:T(2,128)(2,1)} %reshape.699), calls=%async_computation.5 | async-start | bytes 49152 | tf_op jit(solution)/shard_map/all_to_all | solution.py:44
  961.7 15.2 %collective-permute-start.10 = (f32[16,1,144]{0,2,1:T(8,128)}, f32[16,1,144]{0,2,1:T(8,128)}, u32[]{:S(2)}, u32[]{:S(2)}) collective-permute-start(f32[16,1,144]{0,2,1:T(8,128)} %get-tuple-element.22), channel_id=1, source_target_pairs={{0,16},{16,32},{32,48},{48,64},{64,80},{80,96},{96,112},{112,128},... | collective-permute-start | bytes 27656 | tf_op jit(solution)/shard_map/ppermute | solution.py:16
  964.5 15.8 %collective-permute-start.11 = (f32[16,1,144]{0,2,1:T(8,128)S(1)}, f32[16,1,144]{0,2,1:T(8,128)}, u32[]{:S(2)}, u32[]{:S(2)}) collective-permute-start(f32[16,1,144]{0,2,1:T(8,128)S(1)} %get-tuple-element.21), channel_id=1, source_target_pairs={{16,0},{32,16},{48,32},{64,48},{80,64},{96,80},{112,96},{128,112},... | collective-permute-start | bytes 27656 | tf_op jit(solution)/shard_map/ppermute | solution.py:17
